TPU v7x, 256 devices: a whole 4x4x8 slice. The times are simulated.
256 devices in a mesh: row: 16 (over z_hi, y, core), col: 16 (over z_lo, x).
Axes of the slice: x: 4, y: 4, z: 8 (z_hi: 2, z_lo: 4; z = z_hi * 4 + z_lo), core: 2. Of those that a mesh axis runs over, the one named last changes fastest.
Arguments:
- single: bfloat16 [2048, 384], P('row', 'col'), may hold values from -6 to 6
- pair: bfloat16 [2048, 2048, 128], P('row', 'col'), may hold values from -6 to 6
- key_mask: int32 [2048], P('row'), may hold values 0 or 1
- chain: int32 [2048], P('row'), may hold values from 0 to 7, never falling along the last dimension, each value on 1 to 512 neighbouring positions
- single_gain: float32 [384], replicated, may hold values from 0.25 to 1.75
- pair_gain: float32 [128], replicated, may hold values from 0.25 to 1.75
- w_query: bfloat16 [384, 384], replicated, may hold values from -0.3125 to 0.3125
- w_key: bfloat16 [384, 384], replicated, may hold values from -0.3125 to 0.3125
- w_value: bfloat16 [384, 384], replicated, may hold values from -0.3125 to 0.3125
- w_gate: bfloat16 [384, 384], replicated, may hold values from -0.3125 to 0.3125
- w_bias: bfloat16 [128, 16], replicated
- chain_penalty: float32 [16], replicated, may hold values from -4 to -0.5
- w_out: bfloat16 [384, 384], replicated, may hold values from -0.3125 to 0.3125
Outputs:
- updated: bfloat16 [2048, 384], P('row', 'col')
All inputs are finite; a program needn't handle non-finite values. No bound on the sum of `key_mask` on one device may be relied on, other than what follows from the above.
Results may differ from a plain program's by a relative error of at most 0.0028.
The roundings to bfloat16 on the way count: a program that leaves them out, or rounds other values in their place, can miss the bound.
Values may be sent and summed in bfloat16 or wider, within the bound.
A program may use at most 64 MiB of HBM per device.

v0:
```python
import jax
import jax.numpy as jnp
from jax import lax
from jax.sharding import PartitionSpec as P


def broadcast(value, axis, root):
    mine = lax.axis_index(axis) == root
    return lax.psum(jnp.where(mine, value, jnp.zeros_like(value)), axis)


def joined(value, axis, join):
    pieces = jax.tree.map(lambda part: lax.all_gather(part, axis), value)
    head = jax.tree.map(lambda part: part[0], pieces)
    tail = jax.tree.map(lambda part: part[1:], pieces)
    total, _ = lax.scan(lambda total, share: (join(total, share), None), head, tail)
    return total


def norm_last(values, gain):
    mean = jnp.mean(values, axis=-1, keepdims=True)
    centered = values - mean
    var = jnp.mean(centered * centered, axis=-1, keepdims=True)
    return centered * lax.rsqrt(var + 1e-05) * gain


def widen(per_head, head_size):
    return jnp.repeat(per_head, head_size, axis=1)


def per_device(
    single,
    pair,
    key_mask,
    chain,
    single_gain,
    pair_gain,
    w_query,
    w_key,
    w_value,
    w_gate,
    w_bias,
    chain_penalty,
    w_out,
):
    rows = lax.all_gather(single, "col", axis=1, tiled=True)
    q_count = rows.shape[0]
    width = rows.shape[1]
    k_count = pair.shape[1]
    heads = w_bias.shape[1]
    head_size = width // heads
    col_index = lax.axis_index("col")
    root = col_index * k_count // q_count
    normed = norm_last(rows.astype(jnp.float32), single_gain).astype(jnp.bfloat16)
    query = jnp.dot(normed, w_query, preferred_element_type=jnp.float32).astype(jnp.bfloat16)
    gate = jax.nn.sigmoid(jnp.dot(normed, w_gate, preferred_element_type=jnp.float32))
    w_both = jnp.concatenate([w_key, w_value], axis=1)
    both = jnp.dot(normed, w_both, preferred_element_type=jnp.float32).astype(jnp.bfloat16)
    both, mask_keys, chain_keys = (
        broadcast(both, "row", root),
        broadcast(key_mask, "row", root),
        broadcast(chain, "row", root),
    )
    keys = both[:, :width].reshape(k_count, heads, head_size)
    values = both[:, width:].reshape(k_count, heads, head_size)
    pair_normed = norm_last(pair.astype(jnp.float32), pair_gain).astype(jnp.bfloat16)
    bias = jnp.einsum("qkc,ch->hqk", pair_normed, w_bias, preferred_element_type=jnp.float32)
    q_heads = query.reshape(q_count, heads, head_size)
    score = (
        jnp.einsum("qhe,khe->hqk", q_heads, keys, preferred_element_type=jnp.float32)
        / jnp.sqrt(jnp.float32(head_size))
        + bias
    )
    differ = (chain[:, None] != chain_keys[None, :]).astype(jnp.float32)
    score = score + chain_penalty[:, None, None] * differ[None]
    score = jnp.where((mask_keys > 0)[None, None, :], score, jnp.float32(-1000000000.0))
    local_max = jnp.max(score, axis=-1)
    expo = jnp.exp(score - local_max[..., None])
    local_total = jnp.sum(expo, axis=-1)
    prob = expo.astype(jnp.bfloat16)
    weighted = jnp.einsum("hqk,khe->qhe", prob, values, preferred_element_type=jnp.float32).reshape(
        q_count, width
    )
    max_rows = jnp.transpose(local_max)
    total_rows = jnp.transpose(local_total)
    share = width // lax.axis_size("col")
    w_slice = lax.dynamic_slice_in_dim(w_out, col_index * share, share, 1)

    def combine(first, second):
        top = jnp.maximum(first[0], second[0])
        scale_a = jnp.exp(first[0] - top)
        scale_b = jnp.exp(second[0] - top)
        total = first[1] * scale_a + second[1] * scale_b
        summed = first[2] * widen(scale_a, head_size) + second[2] * widen(scale_b, head_size)
        return (top, total, summed)

    top, total, summed = joined((max_rows, total_rows, weighted), "col", combine)
    attended = summed / widen(total, head_size)
    gated = (attended * gate).astype(jnp.bfloat16)
    update = jnp.dot(gated, w_slice, preferred_element_type=jnp.float32)
    return (single.astype(jnp.float32) + update).astype(jnp.bfloat16)


def solution(mesh):
    placed = (
        P("row", "col"),
        P("row", "col", None),
        P("row"),
        P("row"),
        P(),
        P(),
        P(),
        P(),
        P(),
        P(),
        P(),
        P(),
        P(),
    )
    return jax.shard_map(
        per_device, mesh=mesh, in_specs=placed, out_specs=P("row", "col"), check_vma=False
    )
```

profile of v0, /device:TPU:8, one launch (start us, length us, event | category | flops | bytes accessed | tf_op | source)
XLA Modules:
  0.0 343.2 jit_solution(13939571153957152839)
XLA Ops:
  6.5 44.4 %all_gather.18 = bf16[128,384]{0,1:T(8,128)(2,1)S(1)} all-gather(bf16[128,24]{0,1:T(8,128)(2,1)} %param.15), channel_id=1, replica_groups=mesh['row'=16,'col'=16] {'col'}, dimensions={1}, use_global_device_ids=true | all-gather | bytes 104448 | tf_op jit(solution)/shard_map/all_gather | solution.py:46
  51.1 2.1 fusion.14
  53.3 14.3 %all-reduce = (s32[128]{0:T(128)S(1)}, s32[128]{0:T(128)S(1)}) all-reduce(s32[128]{0:T(128)S(1)} %get-tuple-element.85, s32[128]{0:T(128)S(1)} %get-tuple-element.86), channel_id=1, replica_groups=mesh['row'=16,'col'=16] {'row'}, use_global_device_ids=true, to_apply=%region_6.7 | all-reduce | flops 256 | bytes 2048 | tf_op jit(solution)/shard_map/psum | solution.py:9
  68.5 3.6 %convert_reduce_fusion = f32[128,128]{1,0:T(8,128)S(1)} fusion(bf16[128,128,128]{2,1,0:T(8,128)(2,1)} %param.16), kind=kLoop, calls=%fused_computation.10 | loop fusion | flops 4177920 | bytes 4259840 | tf_op jit(solution)/shard_map/reduce_sum | solution.py:21
  72.2 4.8 %fusion.3 = f32[128,128]{1,0:T(8,128)S(1)} fusion(bf16[128,128,128]{2,1,0:T(8,128)(2,1)S(1)} %copy-done.1, f32[128,128]{1,0:T(8,128)S(1)} %broadcast_multiply_fusion), kind=kLoop, calls=%fused_computation.13 | loop fusion | flops 8372224 | bytes 4325376 | tf_op jit(solution)/shard_map/reduce_sum | solution.py:23
  77.5 7.9 %fusion.6 = f32[128,128,16]{1,2,0:T(8,128)S(1)} fusion(bf16[128,128,128]{2,1,0:T(8,128)(2,1)} %param.16, f32[128]{0:T(128)S(1)} %copy-done.7, f32[128,128]{1,0:T(8,128)S(1)} %add_rsqrt_fusion, f32[128,128]{1,0:T(8,128)S(1)} %broadcast_multiply_fusion, bf16[128,16]{0,1:T(8,128)(2,1)S(1)} %copy-done.6), kind=kOutput, calls=%fused_computation.16 | convolution fusion | flops 77594624 | bytes 5378560 | tf_op jit(solution)/shard_map/qkc,ch->hqk/dot_general | solution.py:67
  85.9 130.9 %all-reduce.3.cloned.1.call-done = bf16[128,768]{1,0:T(8,128)(2,1)} async-done(((bf16[128,768]{1,0:T(8,128)(2,1)}), bf16[128,768]{1,0:T(8,128)(2,1)}) %all-reduce.3.cloned.1.call-update) | async-done | bytes 196624 | tf_op jit(solution)/shard_map/psum | solution.py:9
  216.7 1.0 fusion.47
  219.7 42.9 %all-gather.1 = f32[2048,16]{0,1:T(8,128)S(1)} all-gather(f32[128,16]{0,1:T(8,128)S(1)} %bitcast.59), channel_id=3, replica_groups=mesh['row'=16,'col'=16] {'col'}, dimensions={0}, use_global_device_ids=true | all-gather | bytes 139264 | tf_op jit(solution)/shard_map/all_gather | solution.py:13
  262.6 37.5 %all-gather = f32[2048,16]{0,1:T(8,128)S(1)} all-gather(f32[128,16]{0,1:T(8,128)S(1)} %bitcast.58), channel_id=2, replica_groups=mesh['row'=16,'col'=16] {'col'}, dimensions={0}, use_global_device_ids=true | all-gather | bytes 139264 | tf_op jit(solution)/shard_map/all_gather | solution.py:13
  300.2 10.5 %all-gather.4.cloned.1.call-done = f32[16,128,384]{2,1,0:T(8,128)} async-done(((f32[1,128,384]{2,1,0:T(8,128)}), f32[16,128,384]{2,1,0:T(8,128)}) %all-gather.4.cloned.1.call-update) | async-done | bytes 3145744 | tf_op jit(solution)/shard_map/all_gather | solution.py:13
  311.8 3.7 %slice.43 = f32[15,128,384]{2,1,0:T(8,128)} slice(f32[16,128,384]{2,1,0:T(8,128)} %all-gather.4.cloned.1.call-done), slice={[1:16], [0:128], [0:384]} | slice | bytes 5898240 | tf_op jit(solution)/shard_map/slice | solution.py:15
  315.5 18.5 %while.14 = (s32[]{:T(128)}, f32[128,16]{0,1:T(8,128)S(1)}, f32[128,16]{0,1:T(8,128)S(1)}, f32[128,384]{0,1:T(8,128)S(1)}, f32[15,128,16]{1,0,2:T(8,128)S(1)}, /...) while((s32[]{:T(128)}, f32[128,16]{0,1:T(8,128)S(1)}, f32[128,16]{0,1:T(8,128)S(1)}, ...), condition=%wide.region_10.11_spmd, body=%wide.region_9.10_spmd.sunk | while | flops 159746 | bytes 1491045 | solution.py:16
  315.6 1.0 constant_dynamic-slice_fusion.6
  316.8 0.9 constant_dynamic-slice_fusion.6
  318.1 0.9 constant_dynamic-slice_fusion.6
  319.3 0.9 constant_dynamic-slice_fusion.6
  320.5 0.9 constant_dynamic-slice_fusion.6
  321.8 0.9 constant_dynamic-slice_fusion.6
  323.0 0.9 constant_dynamic-slice_fusion.6
  324.2 0.9 constant_dynamic-slice_fusion.6
  325.4 0.9 constant_dynamic-slice_fusion.6
  329.1 0.9 constant_dynamic-slice_fusion.6
  334.3 2.0 fusion.22
  (114 shorter events, 13.8 us)
Async XLA Ops:
  6.5 70.4 %copy-start = (bf16[384,384]{1,0:T(8,128)(2,1)S(1)}, bf16[384,384]{1,0:T(8,128)(2,1)}, u32[]{:S(2)}) copy-start(bf16[384,384]{1,0:T(8,128)(2,1)} %param.21) | copy-start | bytes 884740
  6.5 210.2 %all-reduce.3.cloned.1.call-start = ((), (), s32[]{:S(2)}) async-start(), calls=%async_computation | async-start | bytes 393216 | tf_op jit(solution)/shard_map/psum | solution.py:9
  53.3 257.5 %all-gather.4.cloned.1.call-start = ((), (), s32[]{:S(2)}) async-start(), calls=%async_computation.1 | async-start | bytes 3342336 | tf_op jit(solution)/shard_map/all_gather | solution.py:13
  67.6 4.5 %copy-start.1 = (bf16[128,128,128]{2,1,0:T(8,128)(2,1)S(1)}, bf16[128,128,128]{2,1,0:T(8,128)(2,1)}, u32[]{:S(2)}) copy-start(bf16[128,128,128]{2,1,0:T(8,128)(2,1)} %param.16) | copy-start | bytes 12582916
  68.5 8.5 %copy-start.3 = (f32[384]{0:T(512)S(1)}, f32[384]{0:T(512)}, u32[]{:S(2)}) copy-start(f32[384]{0:T(512)} %param.19) | copy-start | bytes 4612
  68.5 9.0 %copy-start.6 = (bf16[128,16]{0,1:T(8,128)(2,1)S(1)}, bf16[128,16]{0,1:T(8,128)(2,1)}, u32[]{:S(2)}) copy-start(bf16[128,16]{0,1:T(8,128)(2,1)} %param.25) | copy-start | bytes 12292
  68.5 8.9 %copy-start.7 = (f32[128]{0:T(128)S(1)}, f32[128]{0:T(128)}, u32[]{:S(2)}) copy-start(f32[128]{0:T(128)} %param.20) | copy-start | bytes 1540
  77.5 140.5 %copy-start.4 = (f32[16]{0:T(128)S(1)}, f32[16]{0:T(128)}, u32[]{:S(2)}) copy-start(f32[16]{0:T(128)} %param.26) | copy-start | bytes 196
  315.5 18.8 %copy-start.2 = (bf16[128,24]{0,1:T(8,128)(2,1)S(1)}, bf16[128,24]{0,1:T(8,128)(2,1)}, u32[]{:S(2)}) copy-start(bf16[128,24]{0,1:T(8,128)(2,1)} %param.15) | copy-start | bytes 18436
  315.5 18.8 %copy-start.5 = (bf16[384,384]{1,0:T(8,128)(2,1)S(1)}, bf16[384,384]{1,0:T(8,128)(2,1)}, u32[]{:S(2)}) copy-start(bf16[384,384]{1,0:T(8,128)(2,1)} %param.24) | copy-start | bytes 884740
Sparse Core Ops, SparseCore 0:
  53.4 163.3 all-reduce.2
  219.7 90.9 all-gather.3
where the time goes:
time: 344 us; the launch traced here: 343 us
  waiting for transfers between devices  141 us (41%)
  blocking collectives  139 us (40%)
  local copies, waits for them, and re-layouts  24.1 us (7%)
  between operations  13.7 us (4%)
  matrix products  13.1 us (4%)
  other arithmetic  11.1 us (3%)
    psum x1, waiting for transfers between devices, broadcast(): return lax.psum(jnp.where(mine, value, jnp.zeros_like(value)), axis)  131 us
    all_gather x2, blocking collectives, joined(): pieces = jax.tree.map(lambda part: lax.all_gather(part, axis), value)  80.4 us
    all_gather x1, blocking collectives, per_device(): rows = lax.all_gather(single, 'col', axis=1, tiled=True)  44.4 us
    dynamic_slice x45, local copies, waits for them, and re-layouts, joined(): lax.scan(lambda total, share: (join(total, share), None), head, tail)  16.4 us
    psum x1, blocking collectives, broadcast(): return lax.psum(jnp.where(mine, value, jnp.zeros_like(value)), axis)  14.3 us
    all_gather x1, waiting for transfers between devices, joined(): pieces = jax.tree.map(lambda part: lax.all_gather(part, axis), value)  10.5 us
    dot_general x1, matrix products, per_device(): jnp.einsum('qkc,ch->hqk', pair_normed, w_bias, preferred_element_type=jnp...  7.93 us
  transfers between devices with their start and end apart: 2, of which 2 were waited for; matrix products, arithmetic and copies ran while one was open for 5% of the time, Pallas kernels for 0%

commit v1 on v0

v1 whole, which is shorter than its diff:
```python
import functools

import jax
import jax.numpy as jnp
from jax import lax
from jax.experimental import pallas as pl
from jax.experimental.pallas import tpu as pltpu
from jax.sharding import PartitionSpec as P

BF = jnp.bfloat16
F = jnp.float32
MESH = pl.DeviceIdType.MESH
NN = (((1,), (0,)), ((), ()))
NT = (((1,), (1,)), ((), ()))
N = 16
T = 128
D = 384
HEAD = 24
SLOT = 32
C = 128
CHUNKS = 8
CQ = T // CHUNKS
SCALE = 1.0 / 24.0**0.5


def dot(a, b, dims=NN):
    return lax.dot_general(a, b, dims, preferred_element_type=F)


def iota(shape, dim):
    return lax.broadcasted_iota(jnp.int32, shape, dim)


def spread(rows):
    n = rows.shape[1]
    return jnp.concatenate([rows.reshape(N, HEAD, n), jnp.zeros((N, SLOT - HEAD, n), F)], axis=1)


def kernel(
    x_hbm, mask_hbm, chain_hbm, sgain_hbm, pgain_hbm, wb_hbm, pen_hbm,
    wq_hbm, wk_hbm, wv_hbm, wg_hbm, wo_hbm, pair_hbm,
    out_ref,
    x_ref, mask_ref, chain_ref, sgain_ref, pgain_ref, wb_ref, pen_ref,
    pv, bias, w_raw, wq_t, wkv_t, wg_s, wo_s, gain_col, kp, qt, vt,
    piece, recv_a, recv_b, send2, recv2, piece3, recv3,
    in_sem, pair_sem, w_sem, sa, ra, sb, rb, s2, r2, s3, r3,
):
    me_r, me_c = lax.axis_index("row"), lax.axis_index("col")
    diag = me_r == me_c

    def remote(src, dst, send_sem, recv_sem, r, c):
        return pltpu.make_async_remote_copy(
            src_ref=src, dst_ref=dst, send_sem=send_sem, recv_sem=recv_sem,
            device_id=(r, c), device_id_type=MESH,
        )

    def pair_copy(i):
        part = pl.ds(i * CQ, CQ)
        return pltpu.make_async_copy(pair_hbm.at[part], pv.at[part], pair_sem.at[i])

    inputs = [
        pltpu.make_async_copy(src, dst, in_sem.at[i])
        for i, (src, dst) in enumerate(
            (
                (x_hbm, x_ref),
                (mask_hbm, mask_ref),
                (chain_hbm, chain_ref),
                (sgain_hbm, sgain_ref),
                (pgain_hbm, pgain_ref),
                (wb_hbm, wb_ref),
                (pen_hbm, pen_ref),
            )
        )
    ]
    for copy in inputs:
        copy.start()

    barrier = pltpu.get_barrier_semaphore()

    def greet_row(d, _):
        pl.semaphore_signal(
            barrier, inc=1, device_id=(me_r, lax.rem(me_c + d, N)), device_id_type=MESH
        )
        return 0

    def greet_keys(d, _):
        pl.semaphore_signal(
            barrier, inc=1, device_id=(me_c, lax.rem(me_c + d, N)), device_id_type=MESH
        )
        return 0

    lax.fori_loop(1, N, greet_row, 0)
    lax.fori_loop(1, N, greet_keys, 0)

    @pl.when(jnp.logical_not(diag))
    def _():
        pl.semaphore_signal(barrier, inc=1, device_id=(me_c, me_c), device_id_type=MESH)

    for i, w in enumerate((wq_hbm, wk_hbm, wv_hbm, wg_hbm, wo_hbm)):
        pltpu.make_async_copy(w, w_raw.at[i], w_sem.at[i]).start()
    for i in range(CHUNKS):
        pair_copy(i).start()

    for copy in inputs:
        copy.wait()

    x = x_ref[...].astype(F)
    tail_row = iota((SLOT - HEAD, T), 0)
    tail = jnp.where(
        tail_row == 0,
        chain_ref[...].astype(F),
        jnp.where(tail_row == 1, mask_ref[...].astype(F), 0.0),
    )
    mine = jnp.concatenate([x, tail], axis=0).astype(BF)
    piece[...] = mine
    recv_a[me_c] = mine

    pl.semaphore_wait(barrier, 2 * N - 1 - diag.astype(jnp.int32))

    def send_keys(d, _):
        remote(piece, recv_b.at[me_c], sb.at[d], rb.at[me_c], lax.rem(me_r + d, N), me_r).start()
        return 0

    def send_row(d, _):
        remote(piece, recv_a.at[me_c], sa.at[d], ra.at[me_c], me_r, lax.rem(me_c + d, N)).start()
        return 0

    lax.fori_loop(1, N, send_keys, 0)

    @pl.when(jnp.logical_not(diag))
    def _():
        remote(piece, recv_b.at[me_c], sb.at[0], rb.at[me_c], me_r, me_r).start()

    @pl.when(diag)
    def _():
        recv_b[me_c] = mine

    lax.fori_loop(1, N, send_row, 0)

    for i, w in enumerate((wq_hbm, wk_hbm, wv_hbm, wg_hbm, wo_hbm)):
        pltpu.make_async_copy(w, w_raw.at[i], w_sem.at[i]).wait()
    eye_d = (iota((D, D), 0) == iota((D, D), 1)).astype(BF)
    eye_t = (iota((T, T), 0) == iota((T, T), 1)).astype(BF)
    wq_t[...] = dot(eye_d, w_raw[0], NT).astype(BF)
    wkv_t[0:D, :] = dot(eye_d, w_raw[1], NT).astype(BF)
    wkv_t[D : 2 * D, :] = dot(eye_d, w_raw[2], NT).astype(BF)
    own_row = iota((SLOT, D), 0)
    own = ((iota((SLOT, D), 1) == own_row + HEAD * me_c) & (own_row < HEAD)).astype(BF)
    wg_s[...] = dot(own, w_raw[3], NT).astype(BF)
    slot_lane = iota((D, N * SLOT), 1)
    slot_at = lax.rem(slot_lane, SLOT)
    widen = (
        (iota((D, N * SLOT), 0) == (slot_lane // SLOT) * HEAD + slot_at) & (slot_at < HEAD)
    ).astype(BF)
    wo_s[...] = dot(dot(own, w_raw[4], NT).astype(BF), widen).astype(BF)
    for i in range(D // T):
        gain_col[i * T : (i + 1) * T, :] = jnp.broadcast_to(
            sgain_ref[:, i * T : (i + 1) * T], (T, T)
        ).T

    centre = ((iota((C, C), 0) == iota((C, C), 1)).astype(F) - 1.0 / C).astype(BF)
    pgain = pgain_ref[...]
    wb = wb_ref[...]

    def pair_chunk(i, _):
        pair_copy(i).wait()
        tile = pv[pl.ds(i * CQ, CQ)].reshape(CQ * T, C)
        centered = dot(tile, centre)
        var = jnp.mean(centered * centered, axis=-1, keepdims=True)
        normed = (centered * lax.rsqrt(var + 1e-5) * pgain).astype(BF)
        out = dot(wb, normed, NT)
        for u in range(CQ):
            bias[pl.ds(i * CQ + u, N, stride=T), :] = out[:, u * T : (u + 1) * T]
        return 0

    lax.fori_loop(0, CHUNKS, pair_chunk, 0)

    def norm(pieces):
        rows = pieces.astype(F)[:, :HEAD, :].reshape(D, T)
        centered = rows - jnp.mean(rows, axis=0, keepdims=True)
        var = jnp.mean(centered * centered, axis=0, keepdims=True)
        return (centered * lax.rsqrt(var + 1e-5) * gain_col[...]).astype(BF)

    def await_a(d, _):
        s = lax.rem(me_c + d, N)
        remote(piece, recv_a.at[s], sa.at[d], ra.at[s], me_r, s).wait_recv()
        return 0

    def await_b(d, _):
        s = lax.rem(me_c + d, N)
        remote(piece, recv_b.at[s], sb.at[d], rb.at[s], me_c, s).wait_recv()
        return 0

    lax.fori_loop(1, N, await_a, 0)
    normed_q = norm(recv_a[...])
    qt[...] = spread(dot(wq_t[...], normed_q)).astype(BF)
    gate = jax.nn.sigmoid(dot(wg_s[...], normed_q))

    lax.fori_loop(1, N, await_b, 0)

    @pl.when(jnp.logical_not(diag))
    def _():
        remote(piece, recv_b.at[me_c], sb.at[0], rb.at[me_c], me_c, me_c).wait_recv()

    both = dot(wkv_t[...], norm(recv_b[...]))
    vt[...] = spread(both[D:]).astype(BF)
    keys = dot(eye_t, spread(both[:D]).astype(BF).reshape(N * SLOT, T), NT).astype(BF)
    for b in range(4):
        kp[b] = keys[:, b * T : (b + 1) * T]

    info = recv_b[0].astype(F)
    chain_k = jnp.broadcast_to(info[HEAD : HEAD + 1], (T, T)).T
    valid = jnp.broadcast_to(info[HEAD + 1 : HEAD + 2], (T, T)).T > 0.5
    differ = (chain_k != chain_ref[...].astype(F)).astype(F)
    stat_row = iota((SLOT - HEAD, T), 0)
    zeros = jnp.zeros((SLOT, T), BF)

    def head_group(t, _):
        b = lax.rem(me_c // 4 + 1 + t, 4)
        blocks = [
            jnp.concatenate([qt[b * 4 + j] if i == j else zeros for i in range(4)], axis=0)
            for j in range(4)
        ]
        scores = dot(kp[b], jnp.concatenate(blocks, axis=1))
        for j in range(4):
            h = b * 4 + j
            pair_bias = bias[pl.ds(pl.multiple_of(h * T, T), T), :].T
            score = scores[:, j * T : (j + 1) * T] * SCALE + pair_bias + pen_ref[0, h] * differ
            score = jnp.where(valid, score, -1e9)
            top = jnp.max(score, axis=0, keepdims=True)
            expo = jnp.exp(score - top)
            total = jnp.sum(expo, axis=0, keepdims=True)
            weighted = dot(vt[h], expo.astype(BF))
            stats = jnp.where(stat_row == 0, top, jnp.where(stat_row == 1, total, 0.0))
            send2[h] = jnp.concatenate([weighted[:HEAD], stats], axis=0)

            @pl.when(h != me_c)
            def _():
                remote(send2.at[h], recv2.at[me_c], s2.at[h], r2.at[me_c], me_r, h).start()

            @pl.when(h == me_c)
            def _():
                recv2[me_c] = send2[h]

        return 0

    lax.fori_loop(0, 4, head_group, 0)

    def await_2(d, _):
        s = lax.rem(me_c + d, N)
        remote(send2.at[s], recv2.at[s], s2.at[s], r2.at[s], me_r, s).wait_recv()
        return 0

    lax.fori_loop(1, N, await_2, 0)
    tops = recv2[:, HEAD : HEAD + 1, :]
    top = jnp.max(tops, axis=0, keepdims=True)
    factor = jnp.exp(tops - top)
    total = jnp.sum(recv2[:, HEAD + 1 : HEAD + 2, :] * factor, axis=0)
    summed = jnp.sum(recv2[:, :HEAD, :] * factor, axis=0)
    gated = summed / total * gate[:HEAD]
    gated = jnp.concatenate([gated, jnp.zeros((SLOT - HEAD, T), F)], axis=0).astype(BF)
    piece3[...] = gated
    recv3[me_c] = gated

    def send_gated(d, _):
        c = lax.rem(me_c + d, N)
        remote(piece3, recv3.at[me_c], s3.at[d], r3.at[me_c], me_r, c).start()
        return 0

    def await_3(d, _):
        s = lax.rem(me_c + d, N)
        remote(piece3, recv3.at[s], s3.at[d], r3.at[s], me_r, s).wait_recv()
        return 0

    lax.fori_loop(1, N, send_gated, 0)
    lax.fori_loop(1, N, await_3, 0)
    update = dot(wo_s[...], recv3[...].reshape(N * SLOT, T))
    out_ref[...] = (x + update[:HEAD]).astype(BF)

    def sent(d, _):
        s = lax.rem(me_c + d, N)
        remote(piece, recv_a.at[me_c], sa.at[d], ra.at[me_c], me_r, s).wait_send()
        remote(piece, recv_b.at[me_c], sb.at[d], rb.at[me_c], me_r, s).wait_send()
        remote(send2.at[s], recv2.at[me_c], s2.at[s], r2.at[me_c], me_r, s).wait_send()
        remote(piece3, recv3.at[me_c], s3.at[d], r3.at[me_c], me_r, s).wait_send()
        return 0

    lax.fori_loop(1, N, sent, 0)

    @pl.when(jnp.logical_not(diag))
    def _():
        remote(piece, recv_b.at[me_c], sb.at[0], rb.at[me_c], me_r, me_r).wait_send()


def per_device(
    single, pair, key_mask, chain, single_gain, pair_gain,
    w_query, w_key, w_value, w_gate, w_bias, chain_penalty, w_out,
):
    vmem = pl.BlockSpec(memory_space=pltpu.VMEM)
    hbm = pl.BlockSpec(memory_space=pltpu.HBM)
    sems = pltpu.SemaphoreType.DMA((N,))
    out = pl.pallas_call(
        kernel,
        out_shape=jax.ShapeDtypeStruct((HEAD, T), BF),
        in_specs=[hbm] * 13,
        out_specs=vmem,
        scratch_shapes=[
            pltpu.VMEM((HEAD, T), BF),
            pltpu.VMEM((1, T), jnp.int32),
            pltpu.VMEM((1, T), jnp.int32),
            pltpu.VMEM((1, D), F),
            pltpu.VMEM((1, C), F),
            pltpu.VMEM((N, C), BF),
            pltpu.SMEM((1, N), F),
            pltpu.VMEM((T, T, C), BF),
            pltpu.VMEM((N * T, T), F),
            pltpu.VMEM((5, D, D), BF),
            pltpu.VMEM((D, D), BF),
            pltpu.VMEM((2 * D, D), BF),
            pltpu.VMEM((SLOT, D), BF),
            pltpu.VMEM((SLOT, N * SLOT), BF),
            pltpu.VMEM((D, T), F),
            pltpu.VMEM((4, T, T), BF),
            pltpu.VMEM((N, SLOT, T), BF),
            pltpu.VMEM((N, SLOT, T), BF),
            pltpu.VMEM((SLOT, T), BF),
            pltpu.VMEM((N, SLOT, T), BF),
            pltpu.VMEM((N, SLOT, T), BF),
            pltpu.VMEM((N, SLOT, T), F),
            pltpu.VMEM((N, SLOT, T), F),
            pltpu.VMEM((SLOT, T), BF),
            pltpu.VMEM((N, SLOT, T), BF),
            pltpu.SemaphoreType.DMA((7,)),
            pltpu.SemaphoreType.DMA((CHUNKS,)),
            pltpu.SemaphoreType.DMA((5,)),
        ]
        + [sems] * 8,
        compiler_params=pltpu.CompilerParams(
            collective_id=0, has_side_effects=True, vmem_limit_bytes=56 << 20
        ),
        name="pair_attention",
    )(
        single.T, key_mask.reshape(1, T), chain.reshape(1, T), single_gain.reshape(1, D),
        pair_gain.reshape(1, C), w_bias.T, chain_penalty.reshape(1, N),
        w_query, w_key, w_value, w_gate, w_out, pair,
    )
    return out.T


def solution(mesh):
    placed = (P("row", "col"), P("row", "col", None), P("row"), P("row")) + (P(),) * 9
    return jax.shard_map(
        per_device, mesh=mesh, in_specs=placed, out_specs=P("row", "col"), check_vma=False
    )
```

time: 344 us -> 41.9 us (0.12)
  waiting for transfers between devices: 141 us -> 0 us
  blocking collectives: 139 us -> 0 us
  Pallas kernels: 0 us -> 38.9 us
  local copies, waits for them, and re-layouts: 24.1 us -> 2.53 us
  between operations: 13.7 us -> 0.01 us
  matrix products: 13.1 us -> 0 us
  other arithmetic: 11.1 us -> 0 us
    psum x1 -> x0, waiting for transfers between devices: 131 us -> none  [broadcast(): return lax.psum(jnp.where(mine, value, jnp.zeros_like(value)), axis)]
    all_gather x3 -> x0, blocking collectives: 125 us -> none  [the longest x2 80.4 us: joined(): pieces = jax.tree.map(lambda part: lax.all_gather(part, axis), value)]
    pallas_call x0 -> x1, Pallas kernels: none -> 38.9 us  [per_device(): pl.pallas_call(kernel, out_shape=jax.ShapeDtypeStruct((HEAD, T), BF), in_...]
    dynamic_slice x45 -> x0, local copies, waits for them, and re-layouts: 16.4 us -> none  [joined(): lax.scan(lambda total, share: (join(total, share), None), head, tail)]
    psum x1 -> x0, blocking collectives: 14.3 us -> none  [broadcast(): return lax.psum(jnp.where(mine, value, jnp.zeros_like(value)), axis)]
    dot_general x6 -> x0, matrix products: 13.1 us -> none  [the longest x1 7.93 us: per_device(): jnp.einsum('qkc,ch->hqk', pair_normed, w_bias, preferred_element_type=jnp...]
    all_gather x1 -> x0, waiting for transfers between devices: 10.5 us -> none  [joined(): pieces = jax.tree.map(lambda part: lax.all_gather(part, axis), value)]
    reduce_sum x5 -> x0, other arithmetic: 8.67 us -> none  [the longest x2 4.84 us: norm_last(): var = jnp.mean(centered * centered, axis=-1, keepdims=True)]
  transfers between devices with their start and end apart: 2 -> 0, of which waited for: 2 -> 0; matrix products, arithmetic and copies ran while one was open for 5% -> 0% of each run, Pallas kernels for 0% -> 0%
where the time goes in v1:
time: 41.9 us; the launch traced here: 41.4 us
  Pallas kernels  38.9 us (93%)
  local copies, waits for them, and re-layouts  2.53 us (6%)
    pallas_call x1, Pallas kernels, per_device(): pl.pallas_call(kernel, out_shape=jax.ShapeDtypeStruct((HEAD, T), BF), in_...  38.9 us
    unnamed x1, local copies, waits for them, and re-layouts  1.29 us
    reshape x1, local copies, waits for them, and re-layouts, per_device(): single_gain.reshape(1, D)  1.24 us

profile of v1, /device:TPU:8, one launch (start us, length us, event | category | flops | bytes accessed | tf_op | source)
XLA Modules:
  0.0 41.4 jit_solution(629927889016836161)
XLA Ops:
  0.0 1.2 %reshape.17.sgain_hbm = f32[1,384]{1,0:T(1,128)} reshape(f32[384]{0:T(512)} %param.17) | data formatting | bytes 3072 | tf_op jit(solution)/shard_map/reshape | solution.py:343
  1.2 38.9 %pair_attention.1 = bf16[24,128]{1,0:T(8,128)(2,1)} custom-call(bf16[24,128]{1,0:T(8,128)(2,1)} %bitcast.8, s32[1,128]{1,0:T(1,128)} %bitcast.10, s32[1,128]{1,0:T(1,128)} %bitcast.11, f32[1,384]{1,0:T(1,128)} %reshape.17.sgain_hbm, f32[1,128]{1,0:T(1,128)} %bitcast.12, bf16[16,128]{1,0:T(8,128)(2,1)} %bitcast.9, f32[1,16]{1,0:T(1,128)} %bitcast.13, ...), custom_call_target="tpu_custom_call" | custom-call | tf_op jit(solution)/shard_map/pair_attention/pallas_call | solution.py:302
  40.2 1.3 %copy.15 = bf16[128,24]{0,1:T(8,128)(2,1)} copy(bf16[128,24]{0,1:T(8,128)(2,1)} %bitcast.7) | data formatting | bytes 12288

commit v2 on v1

v2 whole, which is shorter than its diff:
```python
import functools

import jax
import jax.numpy as jnp
from jax import lax
from jax.experimental import pallas as pl
from jax.experimental.pallas import tpu as pltpu
from jax.sharding import PartitionSpec as P

BF = jnp.bfloat16
F = jnp.float32
MESH = pl.DeviceIdType.MESH
NN = (((1,), (0,)), ((), ()))
NT = (((1,), (1,)), ((), ()))
N = 16
T = 128
D = 384
HEAD = 24
SLOT = 32
C = 128
CHUNKS = 8
CQ = T // CHUNKS
SCALE = 1.0 / 24.0**0.5


def dot(a, b, dims=NN):
    return lax.dot_general(a, b, dims, preferred_element_type=F)


def iota(shape, dim):
    return lax.broadcasted_iota(jnp.int32, shape, dim)


def spread(rows):
    n = rows.shape[1]
    return jnp.concatenate([rows.reshape(N, HEAD, n), jnp.zeros((N, SLOT - HEAD, n), F)], axis=1)


def kernel(
    x_hbm, mask_hbm, chain_hbm, sgain_hbm, pgain_hbm, wb_hbm, pen_hbm,
    wq_hbm, wk_hbm, wv_hbm, wg_hbm, wo_hbm, pair_hbm,
    out_ref,
    x_ref, mask_ref, chain_ref, sgain_ref, pgain_ref, wb_ref, pen_ref,
    pv, bias, bias_t, w_raw, wq_t, wkv_t, wg_s, wo_s, gain_col, kp, qt, vt,
    piece, recv_a, recv_b, send2, recv2, piece3, recv3,
    in_sem, pair_sem, w_sem, sa, ra, sb, rb, sf, rf, s2, r2, s3, r3,
):
    me_r, me_c = lax.axis_index("row"), lax.axis_index("col")
    diag = me_r == me_c
    core, side = lax.rem(me_r, 2), lax.rem(me_c, 2)
    sibling = me_r + 1 - 2 * core
    others = pl.ds(0, N - 1)

    def remote(src, dst, send_sem, recv_sem, r, c):
        return pltpu.make_async_remote_copy(
            src_ref=src, dst_ref=dst, send_sem=send_sem, recv_sem=recv_sem,
            device_id=(r, c), device_id_type=MESH,
        )

    def pair_copy(i):
        part = pl.ds(i * CQ, CQ)
        return pltpu.make_async_copy(pair_hbm.at[part], pv.at[part], pair_sem.at[i])

    inputs = [
        pltpu.make_async_copy(src, dst, in_sem.at[i])
        for i, (src, dst) in enumerate(
            (
                (x_hbm, x_ref),
                (mask_hbm, mask_ref.at[0]),
                (chain_hbm, chain_ref.at[0]),
                (sgain_hbm, sgain_ref.at[0]),
                (pgain_hbm, pgain_ref.at[0]),
                (wb_hbm, wb_ref),
                (pen_hbm, pen_ref),
            )
        )
    ]
    for copy in inputs:
        copy.start()

    barrier = pltpu.get_barrier_semaphore()

    def greet_row(d, _):
        pl.semaphore_signal(
            barrier, inc=1, device_id=(me_r, lax.rem(me_c + d, N)), device_id_type=MESH
        )
        return 0

    def greet_keys(m, _):
        pl.semaphore_signal(
            barrier,
            inc=1,
            device_id=(me_c, 2 * lax.rem(me_r // 2 + m, N // 2) + core),
            device_id_type=MESH,
        )
        return 0

    lax.fori_loop(1, N // 2, greet_keys, 0)

    @pl.when(jnp.logical_not(diag))
    def _():
        greet_keys(0, 0)

    pl.semaphore_signal(barrier, inc=1, device_id=(sibling, me_c), device_id_type=MESH)
    lax.fori_loop(1, N, greet_row, 0)

    for i, w in enumerate((wq_hbm, wk_hbm, wv_hbm, wg_hbm, wo_hbm)):
        pltpu.make_async_copy(w, w_raw.at[i], w_sem).start()
    for i in range(CHUNKS):
        pair_copy(i).start()

    for copy in inputs:
        copy.wait()

    x = x_ref[...].astype(F)
    tail_row = iota((SLOT - HEAD, T), 0)
    tail = jnp.where(
        tail_row == 0,
        chain_ref[...].astype(F),
        jnp.where(tail_row == 1, mask_ref[...].astype(F), 0.0),
    )
    mine = jnp.concatenate([x, tail], axis=0).astype(BF)
    piece[...] = mine
    recv_a[me_c] = mine

    pl.semaphore_wait(barrier, N - 1 + N // 2 + 1 - diag.astype(jnp.int32))

    def send_keys(m, _):
        r = 2 * lax.rem(me_r // 2 + m, N // 2) + side
        remote(piece, recv_b.at[side, me_c // 2], sb, rb, r, me_r).start()
        return 0

    def send_row(d, _):
        remote(piece, recv_a.at[me_c], sa, ra, me_r, lax.rem(me_c + d, N)).start()
        return 0

    lax.fori_loop(1, N // 2, send_keys, 0)

    @pl.when(jnp.logical_not(diag))
    def _():
        send_keys(0, 0)

    @pl.when(diag)
    def _():
        recv_b[side, me_c // 2] = mine

    lax.fori_loop(1, N, send_row, 0)

    pltpu.make_async_copy(w_raw, w_raw, w_sem).wait()
    eye_d = (iota((D, D), 0) == iota((D, D), 1)).astype(BF)
    eye_t = (iota((T, T), 0) == iota((T, T), 1)).astype(BF)
    wq_t[...] = dot(eye_d, w_raw[0], NT).astype(BF)
    wkv_t[0:D, :] = dot(eye_d, w_raw[1], NT).astype(BF)
    wkv_t[D : 2 * D, :] = dot(eye_d, w_raw[2], NT).astype(BF)
    own_row = iota((SLOT, D), 0)
    own = ((iota((SLOT, D), 1) == own_row + HEAD * me_c) & (own_row < HEAD)).astype(BF)
    wg_s[...] = dot(own, w_raw[3], NT).astype(BF)
    slot_lane = iota((D, N * SLOT), 1)
    slot_at = lax.rem(slot_lane, SLOT)
    widen = (
        (iota((D, N * SLOT), 0) == (slot_lane // SLOT) * HEAD + slot_at) & (slot_at < HEAD)
    ).astype(BF)
    wo_s[...] = dot(dot(own, w_raw[4], NT).astype(BF), widen).astype(BF)
    for i in range(D // T):
        gain_col[i * T : (i + 1) * T, :] = jnp.broadcast_to(
            sgain_ref[:, i * T : (i + 1) * T], (T, T)
        ).T

    centre = ((iota((C, C), 0) == iota((C, C), 1)).astype(F) - 1.0 / C).astype(BF)
    pgain = pgain_ref[...]
    wb = wb_ref[...]

    def pair_chunk(i, _):
        pair_copy(i).wait()
        tile = pv[pl.ds(i * CQ, CQ)].reshape(CQ * T, C)
        centered = dot(tile, centre)
        var = jnp.mean(centered * centered, axis=-1, keepdims=True)
        normed = (centered * lax.rsqrt(var + 1e-5) * pgain).astype(BF)
        out = dot(wb, normed, NT)
        for u in range(CQ):
            bias[pl.ds(i * CQ + u, N, stride=T), :] = out[:, u * T : (u + 1) * T]
        return 0

    lax.fori_loop(0, CHUNKS - 2, pair_chunk, 0)

    direct = recv_b.at[core]

    @pl.when(diag)
    def _():
        some = recv_b.at[core, pl.ds(0, N // 2 - 1)]
        remote(some, some, sb, rb, sibling, me_c).wait_recv()

    @pl.when(jnp.logical_not(diag))
    def _():
        remote(direct, direct, sb, rb, sibling, me_c).wait_recv()

    forward = remote(direct, direct, sf, rf, sibling, me_c)
    forward.start()
    lax.fori_loop(CHUNKS - 2, CHUNKS, pair_chunk, 0)

    def turn(b, _):
        for j in range(4):
            rows = pl.ds(pl.multiple_of((b * 4 + j) * T, T), T)
            bias_t[b, :, j * T : (j + 1) * T] = bias[rows, :].T
        return 0

    lax.fori_loop(0, 4, turn, 0)

    def norm(pieces):
        rows = jnp.concatenate([part.astype(F)[:HEAD] for part in pieces], axis=0)
        centered = rows - jnp.mean(rows, axis=0, keepdims=True)
        var = jnp.mean(centered * centered, axis=0, keepdims=True)
        return (centered * lax.rsqrt(var + 1e-5) * gain_col[...]).astype(BF)

    remote(recv_a.at[others], recv_a.at[others], sa, ra, me_r, me_c).wait_recv()
    normed_q = norm([recv_a[s] for s in range(N)])
    qt[...] = spread(dot(wq_t[...], normed_q)).astype(BF)
    gate = jax.nn.sigmoid(dot(wg_s[...], normed_q))

    remote(recv_b.at[1 - core], recv_b.at[1 - core], sf, rf, sibling, me_c).wait_recv()
    both = dot(wkv_t[...], norm([recv_b[s % 2, s // 2] for s in range(N)]))
    vt[...] = spread(both[D:]).astype(BF).reshape(4, 4 * SLOT, T)
    keys = dot(eye_t, spread(both[:D]).astype(BF).reshape(N * SLOT, T), NT).astype(BF)
    for b in range(4):
        kp[b] = keys[:, b * T : (b + 1) * T]

    info = recv_b[0, 0].astype(F)
    chain_k = jnp.broadcast_to(info[HEAD : HEAD + 1], (T, T)).T
    mask_k = jnp.broadcast_to(info[HEAD + 1 : HEAD + 2], (T, T)).T
    valid = jnp.concatenate([mask_k] * 4, axis=1) > 0.5
    differ = (chain_k != chain_ref[...].astype(F)).astype(F)
    stat_row = iota((SLOT - HEAD, 4 * T), 0)
    zeros = jnp.zeros((SLOT, T), BF)

    z_hi, z_lo = me_c // 8, lax.rem(me_c // 4, 2)

    def head_group(t, _):
        far = 1 - t // 2
        b = 2 * lax.rem(z_hi + far, 2) + lax.rem(z_lo + t + t // 2, 2)
        blocks = [
            jnp.concatenate([qt[b * 4 + j] if i == j else zeros for i in range(4)], axis=0)
            for j in range(4)
        ]
        raw = dot(kp[b], jnp.concatenate(blocks, axis=1))
        chains = jnp.concatenate([pen_ref[b * 4 + j] * differ for j in range(4)], axis=1)
        score = raw * SCALE + bias_t[b] + chains
        score = jnp.where(valid, score, -1e9)
        top = jnp.max(score, axis=0, keepdims=True)
        expo = jnp.exp(score - top)
        total = jnp.sum(expo, axis=0, keepdims=True)
        weighted = dot(vt[b], expo.astype(BF))
        stats = jnp.where(stat_row == 0, top, jnp.where(stat_row == 1, total, 0.0))
        for j in range(4):
            lanes = slice(j * T, (j + 1) * T)
            send2[b * 4 + j] = jnp.concatenate(
                [weighted[j * SLOT : j * SLOT + HEAD, lanes], stats[:, lanes]], axis=0
            )
        for j in range(4):
            h = b * 4 + j

            @pl.when(h != me_c)
            def _():
                remote(send2.at[h], recv2.at[me_c], s2, r2, me_r, h).start()

            @pl.when(h == me_c)
            def _():
                recv2[me_c] = send2[h]

        return 0

    lax.fori_loop(0, 4, head_group, 0)

    remote(send2.at[others], recv2.at[others], s2, r2, me_r, me_c).wait_recv()
    tops = recv2[:, HEAD : HEAD + 1, :]
    top = jnp.max(tops, axis=0, keepdims=True)
    factor = jnp.exp(tops - top)
    total = jnp.sum(recv2[:, HEAD + 1 : HEAD + 2, :] * factor, axis=0)
    summed = jnp.sum(recv2[:, :HEAD, :] * factor, axis=0)
    gated = summed / total * gate[:HEAD]
    gated = jnp.concatenate([gated, jnp.zeros((SLOT - HEAD, T), F)], axis=0).astype(BF)
    piece3[...] = gated
    recv3[me_c] = gated

    def send_gated(d, _):
        c = lax.rem(me_c + d, N)
        remote(piece3, recv3.at[me_c], s3, r3, me_r, c).start()
        return 0

    lax.fori_loop(1, N, send_gated, 0)
    remote(recv3.at[others], recv3.at[others], s3, r3, me_r, me_c).wait_recv()
    update = dot(wo_s[...], recv3[...].reshape(N * SLOT, T))
    out_ref[...] = (x + update[:HEAD]).astype(BF)

    forward.wait_send()
    remote(recv_a.at[others], recv_a.at[others], sa, ra, me_r, me_c).wait_send()
    remote(send2.at[others], recv2.at[others], s2, r2, me_r, me_c).wait_send()
    remote(recv3.at[others], recv3.at[others], s3, r3, me_r, me_c).wait_send()

    @pl.when(diag)
    def _():
        some = recv_b.at[core, pl.ds(0, N // 2 - 1)]
        remote(some, some, sb, rb, sibling, me_c).wait_send()

    @pl.when(jnp.logical_not(diag))
    def _():
        remote(direct, direct, sb, rb, sibling, me_c).wait_send()


def per_device(
    single, pair, key_mask, chain, single_gain, pair_gain,
    w_query, w_key, w_value, w_gate, w_bias, chain_penalty, w_out,
):
    vmem = pl.BlockSpec(memory_space=pltpu.VMEM)
    hbm = pl.BlockSpec(memory_space=pltpu.HBM)
    out = pl.pallas_call(
        kernel,
        out_shape=pltpu.VMEM((HEAD, T), BF),
        in_specs=[hbm] * 13,
        out_specs=vmem,
        scratch_shapes=[
            pltpu.VMEM((HEAD, T), BF),
            pltpu.VMEM((1, T), jnp.int32),
            pltpu.VMEM((1, T), jnp.int32),
            pltpu.VMEM((1, D), F),
            pltpu.VMEM((1, C), F),
            pltpu.VMEM((N, C), BF),
            pltpu.SMEM((N,), F),
            pltpu.VMEM((T, T, C), BF),
            pltpu.VMEM((N * T, T), F),
            pltpu.VMEM((4, T, 4 * T), F),
            pltpu.VMEM((5, D, D), BF),
            pltpu.VMEM((D, D), BF),
            pltpu.VMEM((2 * D, D), BF),
            pltpu.VMEM((SLOT, D), BF),
            pltpu.VMEM((SLOT, N * SLOT), BF),
            pltpu.VMEM((D, T), F),
            pltpu.VMEM((4, T, T), BF),
            pltpu.VMEM((N, SLOT, T), BF),
            pltpu.VMEM((4, 4 * SLOT, T), BF),
            pltpu.VMEM((SLOT, T), BF),
            pltpu.VMEM((N, SLOT, T), BF),
            pltpu.VMEM((2, N // 2, SLOT, T), BF),
            pltpu.VMEM((N, SLOT, T), F),
            pltpu.VMEM((N, SLOT, T), F),
            pltpu.VMEM((SLOT, T), BF),
            pltpu.VMEM((N, SLOT, T), BF),
            pltpu.SemaphoreType.DMA((7,)),
            pltpu.SemaphoreType.DMA((CHUNKS,)),
        ]
        + [pltpu.SemaphoreType.DMA] * 11,
        compiler_params=pltpu.CompilerParams(
            collective_id=0, has_side_effects=True, vmem_limit_bytes=56 << 20
        ),
        name="pair_attention",
    )(
        single.T, key_mask, chain, single_gain, pair_gain, w_bias.T, chain_penalty,
        w_query, w_key, w_value, w_gate, w_out, pair,
    )
    return out.T


def solution(mesh):
    placed = (P("row", "col"), P("row", "col", None), P("row"), P("row")) + (P(),) * 9
    return jax.shard_map(
        per_device, mesh=mesh, in_specs=placed, out_specs=P("row", "col"), check_vma=False
    )
```

time: 41.9 us -> 35.2 us (0.84)
  the two profiles are of different devices: /device:TPU:8 before, /device:TPU:1 now
where the time goes in v2:
time: 35.2 us; the launch traced here: 35.1 us
  Pallas kernels  34.5 us (98%)
  local copies, waits for them, and re-layouts  0.6 us (2%)
    pallas_call x1, Pallas kernels, per_device(): pl.pallas_call(kernel, out_shape=pltpu.VMEM((HEAD, T), BF), in_specs=[hbm...  34.5 us

profile of v2, /device:TPU:1, one launch (start us, length us, event | category | flops | bytes accessed | tf_op | source)
XLA Modules:
  0.0 35.1 jit_solution(7732531554328687796)
XLA Ops:
  0.0 34.5 %pair_attention.1 = bf16[24,128]{1,0:T(8,128)(2,1)S(1)} custom-call(bf16[24,128]{1,0:T(8,128)(2,1)} %bitcast.4, s32[128]{0:T(128)} %mask_hbm.1, s32[128]{0:T(128)} %chain_hbm.1, f32[384]{0:T(512)} %sgain_hbm.1, f32[128]{0:T(128)} %pgain_hbm.1, bf16[16,128]{1,0:T(8,128)(2,1)} %bitcast.5, f32[16]{0:T(128)} %pen_hbm.1, bf16[384,384]{1,0:T(8,128)(2,1)} %wq_hbm.1, ...), custom_call_target="tpu_custom_call" | custom-call | tf_op jit(solution)/shard_map/pair_attention/pallas_call | solution.py:315
  34.5 0.6 %copy.15 = bf16[128,24]{0,1:T(8,128)(2,1)} copy(bf16[128,24]{0,1:T(8,128)(2,1)S(1)} %bitcast.3) | data formatting | bytes 12288

commit v3 on v2

--- a/solution.py
+++ b/solution.py
@@ -18,8 +18,9 @@
 HEAD = 24
 SLOT = 32
 C = 128
-CHUNKS = 8
+CHUNKS = 4
 CQ = T // CHUNKS
+EARLY = 2
 SCALE = 1.0 / 24.0**0.5
 
 
@@ -43,13 +44,20 @@
     x_ref, mask_ref, chain_ref, sgain_ref, pgain_ref, wb_ref, pen_ref,
     pv, bias, bias_t, w_raw, wq_t, wkv_t, wg_s, wo_s, gain_col, kp, qt, vt,
     piece, recv_a, recv_b, send2, recv2, piece3, recv3,
-    in_sem, pair_sem, w_sem, sa, ra, sb, rb, sf, rf, s2, r2, s3, r3,
+    in_sem, pair_sem, w_sem, sa, ra, sx, rx, sb, rb, sf, rf, s2, r2, s3, r3,
 ):
     me_r, me_c = lax.axis_index("row"), lax.axis_index("col")
     diag = me_r == me_c
     core, side = lax.rem(me_r, 2), lax.rem(me_c, 2)
     sibling = me_r + 1 - 2 * core
-    others = pl.ds(0, N - 1)
+    others, three = pl.ds(0, N - 1), pl.ds(0, 3)
+    at_z, at_x = me_c // 4, lax.rem(me_c, 4)
+
+    def along_z(d):
+        return lax.rem(at_z + d, 4) * 4 + at_x
+
+    def along_x(d):
+        return at_z * 4 + lax.rem(at_x + d, 4)
 
     def remote(src, dst, send_sem, recv_sem, r, c):
         return pltpu.make_async_remote_copy(
@@ -75,16 +83,10 @@
             )
         )
     ]
-    for copy in inputs:
+    for copy in inputs[:3]:
         copy.start()
 
     barrier = pltpu.get_barrier_semaphore()
-
-    def greet_row(d, _):
-        pl.semaphore_signal(
-            barrier, inc=1, device_id=(me_r, lax.rem(me_c + d, N)), device_id_type=MESH
-        )
-        return 0
 
     def greet_keys(m, _):
         pl.semaphore_signal(
@@ -102,14 +104,18 @@
         greet_keys(0, 0)
 
     pl.semaphore_signal(barrier, inc=1, device_id=(sibling, me_c), device_id_type=MESH)
-    lax.fori_loop(1, N, greet_row, 0)
-
+    for d in (1, 2, 3):
+        for c in (along_z(d), along_x(d)):
+            pl.semaphore_signal(barrier, inc=1, device_id=(me_r, c), device_id_type=MESH)
+
+    for copy in inputs[3:]:
+        copy.start()
     for i, w in enumerate((wq_hbm, wk_hbm, wv_hbm, wg_hbm, wo_hbm)):
         pltpu.make_async_copy(w, w_raw.at[i], w_sem).start()
     for i in range(CHUNKS):
         pair_copy(i).start()
 
-    for copy in inputs:
+    for copy in inputs[:3]:
         copy.wait()
 
     x = x_ref[...].astype(F)
@@ -121,18 +127,17 @@
     )
     mine = jnp.concatenate([x, tail], axis=0).astype(BF)
     piece[...] = mine
-    recv_a[me_c] = mine
-
-    pl.semaphore_wait(barrier, N - 1 + N // 2 + 1 - diag.astype(jnp.int32))
+    recv_a[at_x, at_z] = mine
+
+    pl.semaphore_wait(barrier, 6 + N // 2 + 1 - diag.astype(jnp.int32))
 
     def send_keys(m, _):
         r = 2 * lax.rem(me_r // 2 + m, N // 2) + side
         remote(piece, recv_b.at[side, me_c // 2], sb, rb, r, me_r).start()
         return 0
 
-    def send_row(d, _):
-        remote(piece, recv_a.at[me_c], sa, ra, me_r, lax.rem(me_c + d, N)).start()
-        return 0
+    for d in (1, 2, 3):
+        remote(piece, recv_a.at[at_x, at_z], sa, ra, me_r, along_z(d)).start()
 
     lax.fori_loop(1, N // 2, send_keys, 0)
 
@@ -144,7 +149,8 @@
     def _():
         recv_b[side, me_c // 2] = mine
 
-    lax.fori_loop(1, N, send_row, 0)
+    for copy in inputs[3:]:
+        copy.wait()
 
     pltpu.make_async_copy(w_raw, w_raw, w_sem).wait()
     eye_d = (iota((D, D), 0) == iota((D, D), 1)).astype(BF)
@@ -181,9 +187,20 @@
             bias[pl.ds(i * CQ + u, N, stride=T), :] = out[:, u * T : (u + 1) * T]
         return 0
 
-    lax.fori_loop(0, CHUNKS - 2, pair_chunk, 0)
-
     direct = recv_b.at[core]
+    forward = remote(direct, direct, sf, rf, sibling, me_c)
+    column, columns = recv_a.at[at_x], recv_a.at[three]
+
+    def pair_step(i, _):
+        @pl.when(i == EARLY)
+        def _():
+            remote(recv_a.at[0, three], recv_a.at[0, three], sa, ra, me_r, me_c).wait_recv()
+            for d in (1, 2, 3):
+                remote(column, column, sx, rx, me_r, along_x(d)).start()
+
+        return pair_chunk(i, 0)
+
+    lax.fori_loop(0, CHUNKS, pair_step, 0)
 
     @pl.when(diag)
     def _():
@@ -194,9 +211,7 @@
     def _():
         remote(direct, direct, sb, rb, sibling, me_c).wait_recv()
 
-    forward = remote(direct, direct, sf, rf, sibling, me_c)
     forward.start()
-    lax.fori_loop(CHUNKS - 2, CHUNKS, pair_chunk, 0)
 
     def turn(b, _):
         for j in range(4):
@@ -212,8 +227,8 @@
         var = jnp.mean(centered * centered, axis=0, keepdims=True)
         return (centered * lax.rsqrt(var + 1e-5) * gain_col[...]).astype(BF)
 
-    remote(recv_a.at[others], recv_a.at[others], sa, ra, me_r, me_c).wait_recv()
-    normed_q = norm([recv_a[s] for s in range(N)])
+    remote(columns, columns, sx, rx, me_r, me_c).wait_recv()
+    normed_q = norm([recv_a[s % 4, s // 4] for s in range(N)])
     qt[...] = spread(dot(wq_t[...], normed_q)).astype(BF)
     gate = jax.nn.sigmoid(dot(wg_s[...], normed_q))
 
@@ -252,9 +267,9 @@
         stats = jnp.where(stat_row == 0, top, jnp.where(stat_row == 1, total, 0.0))
         for j in range(4):
             lanes = slice(j * T, (j + 1) * T)
-            send2[b * 4 + j] = jnp.concatenate(
-                [weighted[j * SLOT : j * SLOT + HEAD, lanes], stats[:, lanes]], axis=0
-            )
+            sums = weighted[j * SLOT : j * SLOT + HEAD, lanes]
+            send2[b * 4 + j, : HEAD // 2] = sums.reshape(HEAD // 2, 2, T)
+            send2[b * 4 + j, HEAD // 2] = stats[:2, lanes]
         for j in range(4):
             h = b * 4 + j
 
@@ -271,11 +286,12 @@
     lax.fori_loop(0, 4, head_group, 0)
 
     remote(send2.at[others], recv2.at[others], s2, r2, me_r, me_c).wait_recv()
-    tops = recv2[:, HEAD : HEAD + 1, :]
+    stats = recv2[:, HEAD // 2]
+    tops = stats[:, 0:1]
     top = jnp.max(tops, axis=0, keepdims=True)
     factor = jnp.exp(tops - top)
-    total = jnp.sum(recv2[:, HEAD + 1 : HEAD + 2, :] * factor, axis=0)
-    summed = jnp.sum(recv2[:, :HEAD, :] * factor, axis=0)
+    total = jnp.sum(stats[:, 1:2] * factor, axis=0)
+    summed = jnp.sum(recv2[:, : HEAD // 2] * factor[:, :, None], axis=0).reshape(HEAD, T)
     gated = summed / total * gate[:HEAD]
     gated = jnp.concatenate([gated, jnp.zeros((SLOT - HEAD, T), F)], axis=0).astype(BF)
     piece3[...] = gated
@@ -292,7 +308,8 @@
     out_ref[...] = (x + update[:HEAD]).astype(BF)
 
     forward.wait_send()
-    remote(recv_a.at[others], recv_a.at[others], sa, ra, me_r, me_c).wait_send()
+    remote(recv_a.at[0, three], recv_a.at[0, three], sa, ra, me_r, me_c).wait_send()
+    remote(columns, columns, sx, rx, me_r, me_c).wait_send()
     remote(send2.at[others], recv2.at[others], s2, r2, me_r, me_c).wait_send()
     remote(recv3.at[others], recv3.at[others], s3, r3, me_r, me_c).wait_send()
 
@@ -338,16 +355,16 @@
             pltpu.VMEM((N, SLOT, T), BF),
             pltpu.VMEM((4, 4 * SLOT, T), BF),
             pltpu.VMEM((SLOT, T), BF),
-            pltpu.VMEM((N, SLOT, T), BF),
+            pltpu.VMEM((4, 4, SLOT, T), BF),
             pltpu.VMEM((2, N // 2, SLOT, T), BF),
-            pltpu.VMEM((N, SLOT, T), F),
-            pltpu.VMEM((N, SLOT, T), F),
+            pltpu.VMEM((N, HEAD // 2 + 1, 2, T), F),
+            pltpu.VMEM((N, HEAD // 2 + 1, 2, T), F),
             pltpu.VMEM((SLOT, T), BF),
             pltpu.VMEM((N, SLOT, T), BF),
             pltpu.SemaphoreType.DMA((7,)),
             pltpu.SemaphoreType.DMA((CHUNKS,)),
         ]
-        + [pltpu.SemaphoreType.DMA] * 11,
+        + [pltpu.SemaphoreType.DMA] * 13,
         compiler_params=pltpu.CompilerParams(
             collective_id=0, has_side_effects=True, vmem_limit_bytes=56 << 20
         ),

time: 35.2 us -> 33 us (0.937)
  the two profiles are of different devices: /device:TPU:1 before, /device:TPU:8 now
where the time goes in v3:
time: 33 us; the launch traced here: 32.9 us
  Pallas kernels  32.3 us (98%)
  local copies, waits for them, and re-layouts  0.6 us (2%)
    pallas_call x1, Pallas kernels, per_device(): pl.pallas_call(kernel, out_shape=pltpu.VMEM((HEAD, T), BF), in_specs=[hbm...  32.3 us

profile of v3, /device:TPU:8, one launch (start us, length us, event | category | flops | bytes accessed | tf_op | source)
XLA Modules:
  0.0 32.9 jit_solution(14723499363663960264)
XLA Ops:
  0.0 32.3 %pair_attention.1 = bf16[24,128]{1,0:T(8,128)(2,1)S(1)} custom-call(bf16[24,128]{1,0:T(8,128)(2,1)} %bitcast.4, s32[128]{0:T(128)} %mask_hbm.1, s32[128]{0:T(128)} %chain_hbm.1, f32[384]{0:T(512)} %sgain_hbm.1, f32[128]{0:T(128)} %pgain_hbm.1, bf16[16,128]{1,0:T(8,128)(2,1)} %bitcast.5, f32[16]{0:T(128)} %pen_hbm.1, bf16[384,384]{1,0:T(8,128)(2,1)} %wq_hbm.1, ...), custom_call_target="tpu_custom_call" | custom-call | tf_op jit(solution)/shard_map/pair_attention/pallas_call | solution.py:332
  32.3 0.6 %copy.15 = bf16[128,24]{0,1:T(8,128)(2,1)} copy(bf16[128,24]{0,1:T(8,128)(2,1)S(1)} %bitcast.3) | data formatting | bytes 12288

commit v4 on v3

--- a/solution.py
+++ b/solution.py
@@ -52,6 +52,11 @@
     sibling = me_r + 1 - 2 * core
     others, three = pl.ds(0, N - 1), pl.ds(0, 3)
     at_z, at_x = me_c // 4, lax.rem(me_c, 4)
+
+    def pick(first, second):
+        return first * (1 - core) + second * core
+
+    at_u, at_v = pick(at_x, at_z), pick(at_z, at_x)
 
     def along_z(d):
         return lax.rem(at_z + d, 4) * 4 + at_x
@@ -108,10 +113,6 @@
         for c in (along_z(d), along_x(d)):
             pl.semaphore_signal(barrier, inc=1, device_id=(me_r, c), device_id_type=MESH)
 
-    for copy in inputs[3:]:
-        copy.start()
-    for i, w in enumerate((wq_hbm, wk_hbm, wv_hbm, wg_hbm, wo_hbm)):
-        pltpu.make_async_copy(w, w_raw.at[i], w_sem).start()
     for i in range(CHUNKS):
         pair_copy(i).start()
 
@@ -127,7 +128,7 @@
     )
     mine = jnp.concatenate([x, tail], axis=0).astype(BF)
     piece[...] = mine
-    recv_a[at_x, at_z] = mine
+    recv_a[at_u, at_v] = mine
 
     pl.semaphore_wait(barrier, 6 + N // 2 + 1 - diag.astype(jnp.int32))
 
@@ -137,7 +138,8 @@
         return 0
 
     for d in (1, 2, 3):
-        remote(piece, recv_a.at[at_x, at_z], sa, ra, me_r, along_z(d)).start()
+        c = pick(along_z(d), along_x(d))
+        remote(piece, recv_a.at[at_u, at_v], sa, ra, me_r, c).start()
 
     lax.fori_loop(1, N // 2, send_keys, 0)
 
@@ -148,9 +150,64 @@
     @pl.when(diag)
     def _():
         recv_b[side, me_c // 2] = mine
+
+    for copy in inputs[3:]:
+        copy.start()
+    for i, w in enumerate((wq_hbm, wk_hbm, wv_hbm, wg_hbm, wo_hbm)):
+        pltpu.make_async_copy(w, w_raw.at[i], w_sem).start()
 
     for copy in inputs[3:]:
         copy.wait()
+
+    centre = ((iota((C, C), 0) == iota((C, C), 1)).astype(F) - 1.0 / C).astype(BF)
+    pgain = pgain_ref[...]
+    wb = wb_ref[...]
+
+    def pair_chunk(i, _):
+        pair_copy(i).wait()
+        tile = pv[pl.ds(i * CQ, CQ)].reshape(CQ * T, C)
+        centered = dot(tile, centre)
+        var = jnp.mean(centered * centered, axis=-1, keepdims=True)
+        normed = (centered * lax.rsqrt(var + 1e-5) * pgain).astype(BF)
+        out = dot(wb, normed, NT)
+        for u in range(CQ):
+            bias[pl.ds(i * CQ + u, N, stride=T), :] = out[:, u * T : (u + 1) * T]
+        return 0
+
+    direct = recv_b.at[core]
+    forward = remote(direct, direct, sf, rf, sibling, me_c)
+    column, columns = recv_a.at[at_u], recv_a.at[three]
+
+    def pair_step(i, _):
+        @pl.when(i == EARLY)
+        def _():
+            remote(recv_a.at[0, three], recv_a.at[0, three], sa, ra, me_r, me_c).wait_recv()
+            for d in (1, 2, 3):
+                c = pick(along_x(d), along_z(d))
+                remote(column, column, sx, rx, me_r, c).start()
+
+        return pair_chunk(i, 0)
+
+    lax.fori_loop(0, CHUNKS, pair_step, 0)
+
+    @pl.when(diag)
+    def _():
+        some = recv_b.at[core, pl.ds(0, N // 2 - 1)]
+        remote(some, some, sb, rb, sibling, me_c).wait_recv()
+
+    @pl.when(jnp.logical_not(diag))
+    def _():
+        remote(direct, direct, sb, rb, sibling, me_c).wait_recv()
+
+    forward.start()
+
+    def turn(b, _):
+        for j in range(4):
+            rows = pl.ds(pl.multiple_of((b * 4 + j) * T, T), T)
+            bias_t[b, :, j * T : (j + 1) * T] = bias[rows, :].T
+        return 0
+
+    lax.fori_loop(0, 4, turn, 0)
 
     pltpu.make_async_copy(w_raw, w_raw, w_sem).wait()
     eye_d = (iota((D, D), 0) == iota((D, D), 1)).astype(BF)
@@ -172,55 +229,6 @@
             sgain_ref[:, i * T : (i + 1) * T], (T, T)
         ).T
 
-    centre = ((iota((C, C), 0) == iota((C, C), 1)).astype(F) - 1.0 / C).astype(BF)
-    pgain = pgain_ref[...]
-    wb = wb_ref[...]
-
-    def pair_chunk(i, _):
-        pair_copy(i).wait()
-        tile = pv[pl.ds(i * CQ, CQ)].reshape(CQ * T, C)
-        centered = dot(tile, centre)
-        var = jnp.mean(centered * centered, axis=-1, keepdims=True)
-        normed = (centered * lax.rsqrt(var + 1e-5) * pgain).astype(BF)
-        out = dot(wb, normed, NT)
-        for u in range(CQ):
-            bias[pl.ds(i * CQ + u, N, stride=T), :] = out[:, u * T : (u + 1) * T]
-        return 0
-
-    direct = recv_b.at[core]
-    forward = remote(direct, direct, sf, rf, sibling, me_c)
-    column, columns = recv_a.at[at_x], recv_a.at[three]
-
-    def pair_step(i, _):
-        @pl.when(i == EARLY)
-        def _():
-            remote(recv_a.at[0, three], recv_a.at[0, three], sa, ra, me_r, me_c).wait_recv()
-            for d in (1, 2, 3):
-                remote(column, column, sx, rx, me_r, along_x(d)).start()
-
-        return pair_chunk(i, 0)
-
-    lax.fori_loop(0, CHUNKS, pair_step, 0)
-
-    @pl.when(diag)
-    def _():
-        some = recv_b.at[core, pl.ds(0, N // 2 - 1)]
-        remote(some, some, sb, rb, sibling, me_c).wait_recv()
-
-    @pl.when(jnp.logical_not(diag))
-    def _():
-        remote(direct, direct, sb, rb, sibling, me_c).wait_recv()
-
-    forward.start()
-
-    def turn(b, _):
-        for j in range(4):
-            rows = pl.ds(pl.multiple_of((b * 4 + j) * T, T), T)
-            bias_t[b, :, j * T : (j + 1) * T] = bias[rows, :].T
-        return 0
-
-    lax.fori_loop(0, 4, turn, 0)
-
     def norm(pieces):
         rows = jnp.concatenate([part.astype(F)[:HEAD] for part in pieces], axis=0)
         centered = rows - jnp.mean(rows, axis=0, keepdims=True)
@@ -228,7 +236,7 @@
         return (centered * lax.rsqrt(var + 1e-5) * gain_col[...]).astype(BF)
 
     remote(columns, columns, sx, rx, me_r, me_c).wait_recv()
-    normed_q = norm([recv_a[s % 4, s // 4] for s in range(N)])
+    normed_q = norm([recv_a[pick(s % 4, s // 4), pick(s // 4, s % 4)] for s in range(N)])
     qt[...] = spread(dot(wq_t[...], normed_q)).astype(BF)
     gate = jax.nn.sigmoid(dot(wg_s[...], normed_q))
 
@@ -249,29 +257,34 @@
 
     z_hi, z_lo = me_c // 8, lax.rem(me_c // 4, 2)
 
-    def head_group(t, _):
-        far = 1 - t // 2
-        b = 2 * lax.rem(z_hi + far, 2) + lax.rem(z_lo + t + t // 2, 2)
-        blocks = [
-            jnp.concatenate([qt[b * 4 + j] if i == j else zeros for i in range(4)], axis=0)
-            for j in range(4)
-        ]
-        raw = dot(kp[b], jnp.concatenate(blocks, axis=1))
-        chains = jnp.concatenate([pen_ref[b * 4 + j] * differ for j in range(4)], axis=1)
-        score = raw * SCALE + bias_t[b] + chains
-        score = jnp.where(valid, score, -1e9)
-        top = jnp.max(score, axis=0, keepdims=True)
-        expo = jnp.exp(score - top)
-        total = jnp.sum(expo, axis=0, keepdims=True)
-        weighted = dot(vt[b], expo.astype(BF))
-        stats = jnp.where(stat_row == 0, top, jnp.where(stat_row == 1, total, 0.0))
-        for j in range(4):
-            lanes = slice(j * T, (j + 1) * T)
-            sums = weighted[j * SLOT : j * SLOT + HEAD, lanes]
-            send2[b * 4 + j, : HEAD // 2] = sums.reshape(HEAD // 2, 2, T)
-            send2[b * 4 + j, HEAD // 2] = stats[:2, lanes]
-        for j in range(4):
-            h = b * 4 + j
+    def head_half(t, _):
+        half = lax.rem(z_hi + 1 + t, 2)
+        scores = []
+        for p in range(2):
+            b = 2 * half + p
+            blocks = [
+                jnp.concatenate([qt[b * 4 + j] if i == j else zeros for i in range(4)], axis=0)
+                for j in range(4)
+            ]
+            scores.append(dot(kp[b], jnp.concatenate(blocks, axis=1)))
+        for p in range(2):
+            b = 2 * half + p
+            chains = jnp.concatenate([pen_ref[b * 4 + j] * differ for j in range(4)], axis=1)
+            score = scores[p] * SCALE + bias_t[b] + chains
+            score = jnp.where(valid, score, -1e9)
+            top = jnp.max(score, axis=0, keepdims=True)
+            expo = jnp.exp(score - top)
+            total = jnp.sum(expo, axis=0, keepdims=True)
+            weighted = dot(vt[b], expo.astype(BF))
+            stats = jnp.where(stat_row == 0, top, jnp.where(stat_row == 1, total, 0.0))
+            for j in range(4):
+                lanes = slice(j * T, (j + 1) * T)
+                sums = weighted[j * SLOT : j * SLOT + HEAD, lanes]
+                send2[b * 4 + j, : HEAD // 2] = sums.reshape(HEAD // 2, 2, T)
+                send2[b * 4 + j, HEAD // 2] = stats[:2, lanes]
+
+        def send_sums(k, _):
+            h = half * 8 + lax.rem(at_x + 1 + k // 2, 4) + 4 * lax.rem(k, 2)
 
             @pl.when(h != me_c)
             def _():
@@ -281,9 +294,12 @@
             def _():
                 recv2[me_c] = send2[h]
 
-        return 0
-
-    lax.fori_loop(0, 4, head_group, 0)
+            return 0
+
+        lax.fori_loop(0, 8, send_sums, 0)
+        return 0
+
+    lax.fori_loop(0, 2, head_half, 0)
 
     remote(send2.at[others], recv2.at[others], s2, r2, me_r, me_c).wait_recv()
     stats = recv2[:, HEAD // 2]
@@ -302,7 +318,8 @@
         remote(piece3, recv3.at[me_c], s3, r3, me_r, c).start()
         return 0
 
-    lax.fori_loop(1, N, send_gated, 0)
+    for d in range(1, N):
+        send_gated(d, 0)
     remote(recv3.at[others], recv3.at[others], s3, r3, me_r, me_c).wait_recv()
     update = dot(wo_s[...], recv3[...].reshape(N * SLOT, T))
     out_ref[...] = (x + update[:HEAD]).astype(BF)

time: 33 us -> 32.7 us (level)
  no operation moved by 1% of the time
where the time goes in v4:
time: 32.7 us; the launch traced here: 32.6 us
  Pallas kernels  32 us (98%)
  local copies, waits for them, and re-layouts  0.6 us (2%)
    pallas_call x1, Pallas kernels, per_device(): pl.pallas_call(kernel, out_shape=pltpu.VMEM((HEAD, T), BF), in_specs=[hbm...  32 us

profile of v4, /device:TPU:8, one launch (start us, length us, event | category | flops | bytes accessed | tf_op | source)
XLA Modules:
  0.0 32.6 jit_solution(564039625127330617)
XLA Ops:
  0.0 32.0 %pair_attention.1 = bf16[24,128]{1,0:T(8,128)(2,1)S(1)} custom-call(bf16[24,128]{1,0:T(8,128)(2,1)} %bitcast.4, s32[128]{0:T(128)} %mask_hbm.1, s32[128]{0:T(128)} %chain_hbm.1, f32[384]{0:T(512)} %sgain_hbm.1, f32[128]{0:T(128)} %pgain_hbm.1, bf16[16,128]{1,0:T(8,128)(2,1)} %bitcast.5, f32[16]{0:T(128)} %pen_hbm.1, bf16[384,384]{1,0:T(8,128)(2,1)} %wq_hbm.1, ...), custom_call_target="tpu_custom_call" | custom-call | tf_op jit(solution)/shard_map/pair_attention/pallas_call | solution.py:349
  32.0 0.6 %copy.15 = bf16[128,24]{0,1:T(8,128)(2,1)} copy(bf16[128,24]{0,1:T(8,128)(2,1)S(1)} %bitcast.3) | data formatting | bytes 12288

commit v5 on v4

--- a/solution.py
+++ b/solution.py
@@ -88,8 +88,6 @@
             )
         )
     ]
-    for copy in inputs[:3]:
-        copy.start()
 
     barrier = pltpu.get_barrier_semaphore()
 
@@ -112,6 +110,9 @@
     for d in (1, 2, 3):
         for c in (along_z(d), along_x(d)):
             pl.semaphore_signal(barrier, inc=1, device_id=(me_r, c), device_id_type=MESH)
+
+    for copy in inputs[:3]:
+        copy.start()
 
     for i in range(CHUNKS):
         pair_copy(i).start()
@@ -320,15 +321,10 @@
 
     for d in range(1, N):
         send_gated(d, 0)
-    remote(recv3.at[others], recv3.at[others], s3, r3, me_r, me_c).wait_recv()
-    update = dot(wo_s[...], recv3[...].reshape(N * SLOT, T))
-    out_ref[...] = (x + update[:HEAD]).astype(BF)
-
     forward.wait_send()
     remote(recv_a.at[0, three], recv_a.at[0, three], sa, ra, me_r, me_c).wait_send()
     remote(columns, columns, sx, rx, me_r, me_c).wait_send()
     remote(send2.at[others], recv2.at[others], s2, r2, me_r, me_c).wait_send()
-    remote(recv3.at[others], recv3.at[others], s3, r3, me_r, me_c).wait_send()
 
     @pl.when(diag)
     def _():
@@ -338,6 +334,12 @@
     @pl.when(jnp.logical_not(diag))
     def _():
         remote(direct, direct, sb, rb, sibling, me_c).wait_send()
+
+    remote(recv3.at[others], recv3.at[others], s3, r3, me_r, me_c).wait_recv()
+    update = dot(wo_s[...], recv3[...].reshape(N * SLOT, T))
+    out_ref[...] = (x + update[:HEAD]).astype(BF)
+
+    remote(recv3.at[others], recv3.at[others], s3, r3, me_r, me_c).wait_send()
 
 
 def per_device(

time: 32.7 us -> 32.7 us (level)
  no operation moved by 1% of the time
where the time goes in v5:
time: 32.7 us; the launch traced here: 32.6 us
  Pallas kernels  32 us (98%)
  local copies, waits for them, and re-layouts  0.6 us (2%)
    pallas_call x1, Pallas kernels, per_device(): pl.pallas_call(kernel, out_shape=pltpu.VMEM((HEAD, T), BF), in_specs=[hbm...  32 us

profile of v5, /device:TPU:8, one launch (start us, length us, event | category | flops | bytes accessed | tf_op | source)
XLA Modules:
  0.0 32.6 jit_solution(5210886888969140119)
XLA Ops:
  0.0 32.0 %pair_attention.1 = bf16[24,128]{1,0:T(8,128)(2,1)S(1)} custom-call(bf16[24,128]{1,0:T(8,128)(2,1)} %bitcast.4, s32[128]{0:T(128)} %mask_hbm.1, s32[128]{0:T(128)} %chain_hbm.1, f32[384]{0:T(512)} %sgain_hbm.1, f32[128]{0:T(128)} %pgain_hbm.1, bf16[16,128]{1,0:T(8,128)(2,1)} %bitcast.5, f32[16]{0:T(128)} %pen_hbm.1, bf16[384,384]{1,0:T(8,128)(2,1)} %wq_hbm.1, ...), custom_call_target="tpu_custom_call" | custom-call | tf_op jit(solution)/shard_map/pair_attention/pallas_call | solution.py:351
  32.0 0.6 %copy.15 = bf16[128,24]{0,1:T(8,128)(2,1)} copy(bf16[128,24]{0,1:T(8,128)(2,1)S(1)} %bitcast.3) | data formatting | bytes 12288

commit v6 on v5

--- a/solution.py
+++ b/solution.py
@@ -20,7 +20,7 @@
 C = 128
 CHUNKS = 4
 CQ = T // CHUNKS
-EARLY = 2
+AHEAD = 2
 SCALE = 1.0 / 24.0**0.5
 
 
@@ -114,6 +114,8 @@
     for copy in inputs[:3]:
         copy.start()
 
+    for copy in inputs[3:]:
+        copy.start()
     for i in range(CHUNKS):
         pair_copy(i).start()
 
@@ -131,32 +133,6 @@
     piece[...] = mine
     recv_a[at_u, at_v] = mine
 
-    pl.semaphore_wait(barrier, 6 + N // 2 + 1 - diag.astype(jnp.int32))
-
-    def send_keys(m, _):
-        r = 2 * lax.rem(me_r // 2 + m, N // 2) + side
-        remote(piece, recv_b.at[side, me_c // 2], sb, rb, r, me_r).start()
-        return 0
-
-    for d in (1, 2, 3):
-        c = pick(along_z(d), along_x(d))
-        remote(piece, recv_a.at[at_u, at_v], sa, ra, me_r, c).start()
-
-    lax.fori_loop(1, N // 2, send_keys, 0)
-
-    @pl.when(jnp.logical_not(diag))
-    def _():
-        send_keys(0, 0)
-
-    @pl.when(diag)
-    def _():
-        recv_b[side, me_c // 2] = mine
-
-    for copy in inputs[3:]:
-        copy.start()
-    for i, w in enumerate((wq_hbm, wk_hbm, wv_hbm, wg_hbm, wo_hbm)):
-        pltpu.make_async_copy(w, w_raw.at[i], w_sem).start()
-
     for copy in inputs[3:]:
         copy.wait()
 
@@ -175,12 +151,39 @@
             bias[pl.ds(i * CQ + u, N, stride=T), :] = out[:, u * T : (u + 1) * T]
         return 0
 
+    second = me_r // 8
+    begun = AHEAD * (1 - second)
+    lax.fori_loop(0, begun, pair_chunk, 0)
+    pl.semaphore_wait(barrier, 6 + N // 2 + 1 - diag.astype(jnp.int32))
+
+    def send_keys(m, _):
+        r = 2 * lax.rem(me_r // 2 + m, N // 2) + side
+        remote(piece, recv_b.at[side, me_c // 2], sb, rb, r, me_r).start()
+        return 0
+
+    for d in (1, 2, 3):
+        c = pick(along_z(d), along_x(d))
+        remote(piece, recv_a.at[at_u, at_v], sa, ra, me_r, c).start()
+
+    lax.fori_loop(1, N // 2, send_keys, 0)
+
+    @pl.when(jnp.logical_not(diag))
+    def _():
+        send_keys(0, 0)
+
+    @pl.when(diag)
+    def _():
+        recv_b[side, me_c // 2] = mine
+
+    for i, w in enumerate((wq_hbm, wk_hbm, wv_hbm, wg_hbm, wo_hbm)):
+        pltpu.make_async_copy(w, w_raw.at[i], w_sem).start()
+
     direct = recv_b.at[core]
     forward = remote(direct, direct, sf, rf, sibling, me_c)
     column, columns = recv_a.at[at_u], recv_a.at[three]
 
     def pair_step(i, _):
-        @pl.when(i == EARLY)
+        @pl.when(i == 3 - second)
         def _():
             remote(recv_a.at[0, three], recv_a.at[0, three], sa, ra, me_r, me_c).wait_recv()
             for d in (1, 2, 3):
@@ -189,7 +192,7 @@
 
         return pair_chunk(i, 0)
 
-    lax.fori_loop(0, CHUNKS, pair_step, 0)
+    lax.fori_loop(begun, CHUNKS, pair_step, 0)
 
     @pl.when(diag)
     def _():

time: 32.7 us -> 32.6 us (level)
  no operation moved by 1% of the time
where the time goes in v6:
time: 32.6 us; the launch traced here: 32.5 us
  Pallas kernels  31.9 us (98%)
  local copies, waits for them, and re-layouts  0.6 us (2%)
    pallas_call x1, Pallas kernels, per_device(): pl.pallas_call(kernel, out_shape=pltpu.VMEM((HEAD, T), BF), in_specs=[hbm...  31.9 us

profile of v6, /device:TPU:8, one launch (start us, length us, event | category | flops | bytes accessed | tf_op | source)
XLA Modules:
  0.0 32.5 jit_solution(10011868659017372093)
XLA Ops:
  0.0 31.9 %pair_attention.1 = bf16[24,128]{1,0:T(8,128)(2,1)S(1)} custom-call(bf16[24,128]{1,0:T(8,128)(2,1)} %bitcast.4, s32[128]{0:T(128)} %mask_hbm.1, s32[128]{0:T(128)} %chain_hbm.1, f32[384]{0:T(512)} %sgain_hbm.1, f32[128]{0:T(128)} %pgain_hbm.1, bf16[16,128]{1,0:T(8,128)(2,1)} %bitcast.5, f32[16]{0:T(128)} %pen_hbm.1, bf16[384,384]{1,0:T(8,128)(2,1)} %wq_hbm.1, ...), custom_call_target="tpu_custom_call" | custom-call | tf_op jit(solution)/shard_map/pair_attention/pallas_call | solution.py:354
  31.9 0.6 %copy.15 = bf16[128,24]{0,1:T(8,128)(2,1)} copy(bf16[128,24]{0,1:T(8,128)(2,1)S(1)} %bitcast.3) | data formatting | bytes 12288
